TPU v7x, 256 devices: a whole 4x4x8 slice. The times are simulated.
256 devices in a mesh: dp: 16 (over z, core), expert: 4 (over y), blk: 4 (over x).
Axes of the slice: x: 4, y: 4, z: 8, core: 2. Of those that a mesh axis runs over, the one named last changes fastest.
Arguments:
- tokens: bfloat16 [2048, 6144], P('dp', 'blk'), may hold values from -6 to 6
- expert_ids: int32 [2048, 2], P('dp'), may hold values from 0 to 7, all different within a row; in each aligned block of 128 rows (0 to 127, 128 to 255, ...) at most 48 rows name the same one
- route_weights: float32 [2048, 2], P('dp'), may hold values from 0.1 to 1
- gate_weight: bfloat16 [8, 6144, 8192], P('expert', 'blk', 'dp'), may hold values from -0.078125 to 0.078125
- up_weight: bfloat16 [8, 6144, 8192], P('expert', 'blk', 'dp'), may hold values from -0.078125 to 0.078125
- down_weight: bfloat16 [8, 8192, 6144], P('expert', 'dp', 'blk'), may hold values from -0.0625 to 0.0625
Outputs:
- mixed: bfloat16 [2048, 6144], P('dp', 'blk')
Inputs may be any that keep to these rules, and one draw needn't show every extreme that they name: `expert_ids`: each row names 2 different experts. Among the 128 rows of one data shard no expert is named more than 48 times, and in every draw some expert is named exactly 48 times in some shard.
All inputs are finite; a program needn't handle non-finite values.
Results may differ from a plain program's by a relative error of at most 0.0051.
Values may be sent and summed in bfloat16 or wider, within the bound.
A program may use at most 64 MiB of HBM per device.

v0:
```python
import jax
import jax.numpy as jnp
from jax import lax
from jax.sharding import PartitionSpec as P

EXPERTS = 8
CAP = 48


def local(tokens, expert_ids, route_weights, gate_weight, up_weight, down_weight):
    local_count = gate_weight.shape[0]
    token_count = tokens.shape[0]
    top_count = expert_ids.shape[1]
    group_index = lax.axis_index("expert")
    flat_ids = expert_ids.reshape(-1)
    one_hot = (flat_ids[:, None] == jnp.arange(EXPERTS, dtype=jnp.int32)[None, :]).astype(jnp.int32)
    before = jnp.cumsum(one_hot, axis=0) - one_hot
    position = jnp.sum(before * one_hot, axis=1)
    local_ids = flat_ids - group_index * local_count
    is_mine = local_ids[:, None] == jnp.arange(local_count, dtype=jnp.int32)[None, :]
    in_slot = position[:, None] == jnp.arange(CAP, dtype=jnp.int32)[None, :]
    slot_hit = (is_mine[:, :, None] & in_slot[:, None, :]).reshape(
        token_count, top_count, local_count, CAP
    )
    dispatch = jnp.any(slot_hit, axis=1).astype(jnp.bfloat16)
    combine = jnp.sum(slot_hit.astype(jnp.float32) * route_weights[:, :, None, None], axis=1)
    picked = jnp.einsum("tec,tf->ecf", dispatch, tokens, preferred_element_type=jnp.float32).astype(
        jnp.bfloat16
    )
    shard_rows = lax.all_gather(picked, "dp", axis=1, tiled=True)
    gate_part = jnp.einsum(
        "enf,efh->enh", shard_rows, gate_weight, preferred_element_type=jnp.float32
    )
    up_part = jnp.einsum("enf,efh->enh", shard_rows, up_weight, preferred_element_type=jnp.float32)
    partial_value = jnp.stack([gate_part, up_part])
    summed = lax.psum(partial_value, "blk")
    hidden = (jax.nn.silu(summed[0]) * summed[1]).astype(jnp.bfloat16)
    expert_out = lax.psum_scatter(
        jnp.einsum("enh,ehd->ned", hidden, down_weight, preferred_element_type=jnp.float32),
        "dp",
        scatter_dimension=0,
        tiled=True,
    )
    mixed_part = jnp.einsum("tec,ced->td", combine, expert_out, precision=lax.Precision.HIGHEST)
    mixed = lax.psum(mixed_part, "expert")
    return mixed.astype(jnp.bfloat16)


def solution(mesh):
    placed = (
        P("dp", "blk"),
        P("dp", None),
        P("dp", None),
        P("expert", "blk", "dp"),
        P("expert", "blk", "dp"),
        P("expert", "dp", "blk"),
    )
    return jax.shard_map(
        local, mesh=mesh, in_specs=placed, out_specs=P("dp", "blk"), check_vma=False
    )
```

profile of v0, /device:TPU:2, one launch (start us, length us, event | category | flops | bytes accessed | tf_op | source)
XLA Modules:
  0.0 316.2 jit_solution(18314517861227424447)
XLA Ops:
  6.5 0.9 copy.13
  7.5 0.1 eq.65
  7.6 0.1 reshape.70
  7.8 0.6 reduce-window.6
  8.4 0.2 slice_reduce_fusion
  8.6 0.1 fusion.7
  8.7 0.1 eq.69
  8.9 0.1 copy.15
  9.0 0.7 broadcast_subtract_fusion
  9.7 1.9 convolution_convert_fusion
  11.7 0.0 all-reduce.3.cloned.1.call-start
  11.7 45.8 %all-gather.2.cloned.1.call-done = bf16[2,768,1536]{2,1,0:T(8,128)(2,1)} async-done(((bf16[2,48,1536]{2,1,0:T(8,128)(2,1)}), bf16[2,768,1536]{2,1,0:T(8,128)(2,1)}) %all-gather.2.cloned.1.call-update) | async-done | bytes 4718608 | tf_op jit(solution)/shard_map/all_gather | solution.py:30
  57.5 5.5 %convolution_bitcast_fusion.2 = f32[1,2,768,512]{3,2,1,0:T(8,128)S(1)} fusion(bf16[2,768,1536]{2,1,0:T(8,128)(2,1)} %all-gather.2.cloned.1.call-done, bf16[2,1536,512]{2,1,0:T(8,128)(2,1)} %param.10), kind=kOutput, calls=%fused_computation.8 | convolution fusion | flops 2415919104 | bytes 11010048 | tf_op jit(solution)/shard_map/enf,efh->enh/dot_general | solution.py:34
  63.0 0.1 copy-done.3
  63.1 2.6 convolution_bitcast_fusion.3
  65.7 3.4 %pad_maximum_fusion = f32[2,2,768,512]{3,2,1,0:T(8,128)} fusion(f32[1,2,768,512]{3,2,1,0:T(8,128)S(1)} %convolution_bitcast_fusion.2, f32[1,2,768,512]{3,2,1,0:T(8,128)S(1)} %convolution_bitcast_fusion.3), kind=kLoop, calls=%fused_computation | loop fusion | flops 1572864 | bytes 12582912 | tf_op jit(solution)/shard_map/stack | solution.py:35
  69.1 0.0 all-reduce.3.cloned.1.call-update
  69.1 0.0 reduce-scatter.2.cloned.1.call-start
  69.1 129.7 %all-reduce.3.cloned.1.call-done = f32[2,2,768,512]{3,2,1,0:T(8,128)} async-done(((f32[2,2,768,512]{3,2,1,0:T(8,128)}), f32[2,2,768,512]{3,2,1,0:T(8,128)}) %all-reduce.3.cloned.1.call-update) | async-done | bytes 6291472 | tf_op jit(solution)/shard_map/psum | solution.py:36
  198.9 8.0 %convolution_bitcast_fusion = f32[768,2,1536]{2,0,1:T(8,128)} fusion(bf16[2,512,1536]{2,1,0:T(8,128)(2,1)S(1)} %copy-done, f32[2,2,768,512]{3,2,1,0:T(8,128)} %all-reduce.3.cloned.1.call-done), kind=kOutput, calls=%fused_computation.1 | convolution fusion | flops 2420637696 | bytes 18874368 | tf_op jit(solution)/shard_map/enh,ehd->ned/dot_general | solution.py:39
  206.9 0.7 copy-done.1
  207.6 73.1 %reduce-scatter.2.cloned.1.call-done = f32[48,2,1536]{2,0,1:T(8,128)} async-done(((f32[768,2,1536]{2,0,1:T(8,128)}), f32[48,2,1536]{2,0,1:T(8,128)}) %reduce-scatter.2.cloned.1.call-update) | async-done | bytes 589840 | tf_op jit(solution)/shard_map/reduce_scatter | solution.py:38
  280.7 2.8 convolution_bitcast_fusion.1
  283.5 26.3 %all-reduce.4 = bf16[128,1536]{1,0:T(8,128)(2,1)} all-reduce(f32[128,1536]{1,0:T(8,128)} %convolution_bitcast_fusion.1), channel_id=1, replica_groups=mesh['dp'=16,'expert'=4,'blk'=4] {'expert'}, use_global_device_ids=true, to_apply=%region_7.8 | all-reduce | flops 196608 | bytes 1179648 | tf_op jit(solution)/shard_map/psum | solution.py:45
  (16 shorter events, 0.2 us)
Async XLA Ops:
  6.5 192.3 %copy-start = (bf16[2,512,1536]{2,1,0:T(8,128)(2,1)S(1)}, bf16[2,512,1536]{2,1,0:T(8,128)(2,1)}, u32[]{:S(2)}) copy-start(bf16[2,512,1536]{2,1,0:T(8,128)(2,1)} %param.11) | copy-start | bytes 9437188
  6.5 50.9 %all-gather.2.cloned.1.call-start = ((), (), s32[]{:S(2)}) async-start(), calls=%async_computation.1 | async-start | bytes 5013504 | tf_op jit(solution)/shard_map/all_gather | solution.py:30
  11.7 187.2 %all-reduce.3.cloned.1.call-start = ((), (), s32[]{:S(2)}) async-start(), calls=%async_computation.2 | async-start | bytes 12582912 | tf_op jit(solution)/shard_map/psum | solution.py:36
  57.5 5.6 %copy-start.2 = (bf16[2,768,1536]{2,1,0:T(8,128)(2,1)S(1)}, bf16[2,768,1536]{2,1,0:T(8,128)(2,1)}, u32[]{:S(2)}) copy-start(bf16[2,768,1536]{2,1,0:T(8,128)(2,1)} %all-gather.2.cloned.1.call-done) | copy-start | bytes 14155780
  57.5 5.6 %copy-start.3 = (bf16[2,1536,512]{2,1,0:T(8,128)(2,1)S(1)}, bf16[2,1536,512]{2,1,0:T(8,128)(2,1)}, u32[]{:S(2)}) copy-start(bf16[2,1536,512]{2,1,0:T(8,128)(2,1)} %param.9) | copy-start | bytes 9437188
  69.1 211.6 %reduce-scatter.2.cloned.1.call-start = ((), (), s32[]{:S(2)}) async-start(), calls=%async_computation.3 | async-start | bytes 10027008 | tf_op jit(solution)/shard_map/reduce_scatter | solution.py:38
  206.9 0.7 copy-start.1
Sparse Core Ops, SparseCore 0:
  11.8 45.6 all-gather.1
  69.2 129.6 all-reduce.2
  207.0 73.5 reduce-scatter.1
where the time goes:
time: 316 us
  waiting for transfers between devices  249 us (79%)
  blocking collectives  26.3 us (8%)
  matrix products  20.9 us (7%)
  between operations  13.2 us (4%)
  other arithmetic  4.85 us (2%)
    psum x1, waiting for transfers between devices, local(): summed = lax.psum(partial_value, 'blk')  130 us
    reduce_scatter x1, waiting for transfers between devices, local(): lax.psum_scatter(jnp.einsum('enh,ehd->ned', hidden, down_weight, preferre...  73.1 us
    all_gather x1, waiting for transfers between devices, local(): shard_rows = lax.all_gather(picked, 'dp', axis=1, tiled=True)  45.8 us
    psum x1, blocking collectives, local(): mixed = lax.psum(mixed_part, 'expert')  26.3 us
    dot_general x1, matrix products, local(): jnp.einsum('enh,ehd->ned', hidden, down_weight, preferred_element_type=jn...  8.03 us
  transfers between devices with their start and end apart: 3, of which 3 were waited for; matrix products, arithmetic and copies ran while one was open for 0% of the time, Pallas kernels for 0%

commit v1 on v0

--- a/solution.py
+++ b/solution.py
@@ -27,7 +27,14 @@
     picked = jnp.einsum("tec,tf->ecf", dispatch, tokens, preferred_element_type=jnp.float32).astype(
         jnp.bfloat16
     )
-    shard_rows = lax.all_gather(picked, "dp", axis=1, tiled=True)
+    size = lax.axis_size("dp")
+    route = [(i, (i + 1) % size) for i in range(size)]
+    pieces = [picked]
+    for far in range(1, size):
+        pieces = [lax.ppermute(pieces[0], "dp", route), *pieces]
+    full = jnp.concatenate(pieces, axis=1)
+    shift = (lax.axis_index("dp") + 1) * pieces[-1].shape[1]
+    shard_rows = jnp.roll(full, shift, axis=1)
     gate_part = jnp.einsum(
         "enf,efh->enh", shard_rows, gate_weight, preferred_element_type=jnp.float32
     )

time: 316 us -> 410 us (1.30)
  waiting for transfers between devices: 249 us -> 318 us
  local copies, waits for them, and re-layouts: 2.37 us -> 28.7 us
    ppermute x0 -> x15, waiting for transfers between devices: none -> 113 us  [local(): pieces = [lax.ppermute(pieces[0], 'dp', route), *pieces]]
    all_gather x1 -> x0, waiting for transfers between devices: 45.8 us -> none  [local(): shard_rows = lax.all_gather(picked, 'dp', axis=1, tiled=True)]
    unnamed x9 -> x92, local copies, waits for them, and re-layouts: 1.67 us -> 28 us
  transfers between devices with their start and end apart: 3 -> 17, of which waited for: 3 -> 17; matrix products, arithmetic and copies ran while one was open for 0% -> 0% of each run, Pallas kernels for 0% -> 0%
where the time goes in v1:
time: 410 us; the launch traced here: 409 us
  waiting for transfers between devices  318 us (78%)
  local copies, waits for them, and re-layouts  28.7 us (7%)
  blocking collectives  26.2 us (6%)
  matrix products  17.3 us (4%)
  between operations  13.9 us (3%)
  other arithmetic  4.85 us (1%)
    psum x1, waiting for transfers between devices, local(): summed = lax.psum(partial_value, 'blk')  132 us
    ppermute x15, waiting for transfers between devices, local(): pieces = [lax.ppermute(pieces[0], 'dp', route), *pieces]  113 us
    reduce_scatter x1, waiting for transfers between devices, local(): lax.psum_scatter(jnp.einsum('enh,ehd->ned', hidden, down_weight, preferre...  73.1 us
    unnamed x92, local copies, waits for them, and re-layouts  28 us
    psum x1, blocking collectives, local(): mixed = lax.psum(mixed_part, 'expert')  26.2 us
  transfers between devices with their start and end apart: 17, of which 17 were waited for; matrix products, arithmetic and copies ran while one was open for 0% of the time, Pallas kernels for 0%

profile of v1, /device:TPU:2, one launch (start us, length us, event | category | flops | bytes accessed | tf_op | source)
XLA Modules:
  0.0 408.9 jit_solution(7172568804399719344)
XLA Ops:
  9.7 1.2 convolution_convert_fusion
  10.9 9.7 %collective-permute-done = bf16[2,48,1536]{2,1,0:T(8,128)(2,1)S(1)} collective-permute-done((bf16[2,48,1536]{2,1,0:T(8,128)(2,1)S(1)}, bf16[2,48,1536]{2,1,0:T(8,128)(2,1)S(1)}, u32[]{:S(2)}, u32[]{:S(2)}) %collective-permute-start) | collective-permute-done | bytes 294944 | tf_op jit(solution)/shard_map/ppermute | solution.py:34
  21.3 7.4 %collective-permute-done.1 = bf16[2,48,1536]{2,1,0:T(8,128)(2,1)S(1)} collective-permute-done((bf16[2,48,1536]{2,1,0:T(8,128)(2,1)S(1)}, bf16[2,48,1536]{2,1,0:T(8,128)(2,1)S(1)}, u32[]{:S(2)}, u32[]{:S(2)}) %collective-permute-start.1) | collective-permute-done | bytes 294944 | tf_op jit(solution)/shard_map/ppermute | solution.py:34
  29.4 7.4 %collective-permute-done.2 = bf16[2,48,1536]{2,1,0:T(8,128)(2,1)S(1)} collective-permute-done((bf16[2,48,1536]{2,1,0:T(8,128)(2,1)S(1)}, bf16[2,48,1536]{2,1,0:T(8,128)(2,1)S(1)}, u32[]{:S(2)}, u32[]{:S(2)}) %collective-permute-start.2) | collective-permute-done | bytes 294944 | tf_op jit(solution)/shard_map/ppermute | solution.py:34
  37.5 7.4 %collective-permute-done.3 = bf16[2,48,1536]{2,1,0:T(8,128)(2,1)S(1)} collective-permute-done((bf16[2,48,1536]{2,1,0:T(8,128)(2,1)S(1)}, bf16[2,48,1536]{2,1,0:T(8,128)(2,1)S(1)}, u32[]{:S(2)}, u32[]{:S(2)}) %collective-permute-start.3) | collective-permute-done | bytes 294944 | tf_op jit(solution)/shard_map/ppermute | solution.py:34
  45.6 7.4 %collective-permute-done.4 = bf16[2,48,1536]{2,1,0:T(8,128)(2,1)S(1)} collective-permute-done((bf16[2,48,1536]{2,1,0:T(8,128)(2,1)S(1)}, bf16[2,48,1536]{2,1,0:T(8,128)(2,1)S(1)}, u32[]{:S(2)}, u32[]{:S(2)}) %collective-permute-start.4) | collective-permute-done | bytes 294944 | tf_op jit(solution)/shard_map/ppermute | solution.py:34
  53.7 7.4 %collective-permute-done.5 = bf16[2,48,1536]{2,1,0:T(8,128)(2,1)S(1)} collective-permute-done((bf16[2,48,1536]{2,1,0:T(8,128)(2,1)S(1)}, bf16[2,48,1536]{2,1,0:T(8,128)(2,1)S(1)}, u32[]{:S(2)}, u32[]{:S(2)}) %collective-permute-start.5) | collective-permute-done | bytes 294944 | tf_op jit(solution)/shard_map/ppermute | solution.py:34
  61.7 7.4 %collective-permute-done.6 = bf16[2,48,1536]{2,1,0:T(8,128)(2,1)S(1)} collective-permute-done((bf16[2,48,1536]{2,1,0:T(8,128)(2,1)S(1)}, bf16[2,48,1536]{2,1,0:T(8,128)(2,1)S(1)}, u32[]{:S(2)}, u32[]{:S(2)}) %collective-permute-start.6) | collective-permute-done | bytes 294944 | tf_op jit(solution)/shard_map/ppermute | solution.py:34
  69.8 7.4 %collective-permute-done.7 = bf16[2,48,1536]{2,1,0:T(8,128)(2,1)S(1)} collective-permute-done((bf16[2,48,1536]{2,1,0:T(8,128)(2,1)S(1)}, bf16[2,48,1536]{2,1,0:T(8,128)(2,1)S(1)}, u32[]{:S(2)}, u32[]{:S(2)}) %collective-permute-start.7) | collective-permute-done | bytes 294944 | tf_op jit(solution)/shard_map/ppermute | solution.py:34
  77.9 7.4 %collective-permute-done.8 = bf16[2,48,1536]{2,1,0:T(8,128)(2,1)S(1)} collective-permute-done((bf16[2,48,1536]{2,1,0:T(8,128)(2,1)S(1)}, bf16[2,48,1536]{2,1,0:T(8,128)(2,1)S(1)}, u32[]{:S(2)}, u32[]{:S(2)}) %collective-permute-start.8) | collective-permute-done | bytes 294944 | tf_op jit(solution)/shard_map/ppermute | solution.py:34
  86.0 7.4 %collective-permute-done.9 = bf16[2,48,1536]{2,1,0:T(8,128)(2,1)S(1)} collective-permute-done((bf16[2,48,1536]{2,1,0:T(8,128)(2,1)S(1)}, bf16[2,48,1536]{2,1,0:T(8,128)(2,1)S(1)}, u32[]{:S(2)}, u32[]{:S(2)}) %collective-permute-start.9) | collective-permute-done | bytes 294944 | tf_op jit(solution)/shard_map/ppermute | solution.py:34
  94.1 7.4 %collective-permute-done.10 = bf16[2,48,1536]{2,1,0:T(8,128)(2,1)S(1)} collective-permute-done((bf16[2,48,1536]{2,1,0:T(8,128)(2,1)S(1)}, bf16[2,48,1536]{2,1,0:T(8,128)(2,1)S(1)}, u32[]{:S(2)}, u32[]{:S(2)}) %collective-permute-start.10) | collective-permute-done | bytes 294944 | tf_op jit(solution)/shard_map/ppermute | solution.py:34
  102.1 7.4 %collective-permute-done.11 = bf16[2,48,1536]{2,1,0:T(8,128)(2,1)S(1)} collective-permute-done((bf16[2,48,1536]{2,1,0:T(8,128)(2,1)S(1)}, bf16[2,48,1536]{2,1,0:T(8,128)(2,1)S(1)}, u32[]{:S(2)}, u32[]{:S(2)}) %collective-permute-start.11) | collective-permute-done | bytes 294944 | tf_op jit(solution)/shard_map/ppermute | solution.py:34
  110.2 7.4 %collective-permute-done.12 = bf16[2,48,1536]{2,1,0:T(8,128)(2,1)S(1)} collective-permute-done((bf16[2,48,1536]{2,1,0:T(8,128)(2,1)S(1)}, bf16[2,48,1536]{2,1,0:T(8,128)(2,1)S(1)}, u32[]{:S(2)}, u32[]{:S(2)}) %collective-permute-start.12) | collective-permute-done | bytes 294944 | tf_op jit(solution)/shard_map/ppermute | solution.py:34
  118.3 7.5 %collective-permute-done.13 = bf16[2,48,1536]{2,1,0:T(8,128)(2,1)} collective-permute-done((bf16[2,48,1536]{2,1,0:T(8,128)(2,1)S(1)}, bf16[2,48,1536]{2,1,0:T(8,128)(2,1)}, u32[]{:S(2)}, u32[]{:S(2)}) %collective-permute-start.13) | collective-permute-done | bytes 294944 | tf_op jit(solution)/shard_map/ppermute | solution.py:34
  125.9 7.5 %collective-permute-done.14 = bf16[2,48,1536]{2,1,0:T(8,128)(2,1)} collective-permute-done((bf16[2,48,1536]{2,1,0:T(8,128)(2,1)}, bf16[2,48,1536]{2,1,0:T(8,128)(2,1)}, u32[]{:S(2)}, u32[]{:S(2)}) %collective-permute-start.14) | collective-permute-done | bytes 294944 | tf_op jit(solution)/shard_map/ppermute | solution.py:34
  150.8 2.6 fusion.6
  153.4 2.6 fusion.9
  156.0 3.4 pad_maximum_fusion
  159.4 131.7 %all-reduce.3.cloned.1.call-done = f32[2,2,768,512]{3,2,1,0:T(8,128)} async-done(((f32[2,2,768,512]{3,2,1,0:T(8,128)}), f32[2,2,768,512]{3,2,1,0:T(8,128)}) %all-reduce.3.cloned.1.call-update) | async-done | bytes 6291472 | tf_op jit(solution)/shard_map/psum | solution.py:43
  291.1 8.1 %convolution_bitcast_fusion = f32[768,2,1536]{2,0,1:T(8,128)} fusion(bf16[2,512,1536]{2,1,0:T(8,128)(2,1)S(1)} %copy-done, f32[2,2,768,512]{3,2,1,0:T(8,128)} %all-reduce.3.cloned.1.call-done), kind=kOutput, calls=%fused_computation.1 | convolution fusion | flops 2420637696 | bytes 18874368 | tf_op jit(solution)/shard_map/enh,ehd->ned/dot_general | solution.py:46
  299.9 73.1 %reduce-scatter.2.cloned.1.call-done = f32[48,2,1536]{2,0,1:T(8,128)} async-done(((f32[768,2,1536]{2,0,1:T(8,128)}), f32[48,2,1536]{2,0,1:T(8,128)}) %reduce-scatter.2.cloned.1.call-update) | async-done | bytes 589840 | tf_op jit(solution)/shard_map/reduce_scatter | solution.py:45
  373.0 2.8 convolution_bitcast_fusion.1
  375.8 26.2 %all-reduce.4 = bf16[128,1536]{1,0:T(8,128)(2,1)} all-reduce(f32[128,1536]{1,0:T(8,128)} %convolution_bitcast_fusion.1), channel_id=1, replica_groups=mesh['dp'=16,'expert'=4,'blk'=4] {'expert'}, use_global_device_ids=true, to_apply=%region_7.8 | all-reduce | flops 196608 | bytes 1179648 | tf_op jit(solution)/shard_map/psum | solution.py:52
  (127 shorter events, 30.3 us)
Async XLA Ops:
  6.5 284.6 %copy-start = (bf16[2,512,1536]{2,1,0:T(8,128)(2,1)S(1)}, bf16[2,512,1536]{2,1,0:T(8,128)(2,1)}, u32[]{:S(2)}) copy-start(bf16[2,512,1536]{2,1,0:T(8,128)(2,1)} %param.11) | copy-start | bytes 9437188
  6.5 284.6 %all-reduce.3.cloned.1.call-start = ((), (), s32[]{:S(2)}) async-start(), calls=%async_computation.1 | async-start | bytes 12582912 | tf_op jit(solution)/shard_map/psum | solution.py:43
  10.9 9.7 %collective-permute-start = (bf16[2,48,1536]{2,1,0:T(8,128)(2,1)S(1)}, bf16[2,48,1536]{2,1,0:T(8,128)(2,1)S(1)}, u32[]{:S(2)}, u32[]{:S(2)}) collective-permute-start(bf16[2,48,1536]{2,1,0:T(8,128)(2,1)S(1)} %convolution_convert_fusion), channel_id=1, source_target_pairs={{0,16},{16,32},{32,48},{48,64},{64,80},{80,96},{96,112},{112,128},... | collective-permute-start | bytes 884744 | tf_op jit(solution)/shard_map/ppermute | solution.py:34
  21.3 7.4 %collective-permute-start.1 = (bf16[2,48,1536]{2,1,0:T(8,128)(2,1)S(1)}, bf16[2,48,1536]{2,1,0:T(8,128)(2,1)S(1)}, u32[]{:S(2)}, u32[]{:S(2)}) collective-permute-start(bf16[2,48,1536]{2,1,0:T(8,128)(2,1)S(1)} %collective-permute-done), channel_id=1, source_target_pairs={{0,16},{16,32},{32,48},{48,64},{64,80},{80,96},{96,112},{112,128},... | collective-permute-start | bytes 884744 | tf_op jit(solution)/shard_map/ppermute | solution.py:34
  29.4 7.4 %collective-permute-start.2 = (bf16[2,48,1536]{2,1,0:T(8,128)(2,1)S(1)}, bf16[2,48,1536]{2,1,0:T(8,128)(2,1)S(1)}, u32[]{:S(2)}, u32[]{:S(2)}) collective-permute-start(bf16[2,48,1536]{2,1,0:T(8,128)(2,1)S(1)} %collective-permute-done.1), channel_id=1, source_target_pairs={{0,16},{16,32},{32,48},{48,64},{64,80},{80,96},{96,112},{112,128},... | collective-permute-start | bytes 884744 | tf_op jit(solution)/shard_map/ppermute | solution.py:34
  37.5 7.4 %collective-permute-start.3 = (bf16[2,48,1536]{2,1,0:T(8,128)(2,1)S(1)}, bf16[2,48,1536]{2,1,0:T(8,128)(2,1)S(1)}, u32[]{:S(2)}, u32[]{:S(2)}) collective-permute-start(bf16[2,48,1536]{2,1,0:T(8,128)(2,1)S(1)} %collective-permute-done.2), channel_id=1, source_target_pairs={{0,16},{16,32},{32,48},{48,64},{64,80},{80,96},{96,112},{112,128},... | collective-permute-start | bytes 884744 | tf_op jit(solution)/shard_map/ppermute | solution.py:34
  45.6 7.4 %collective-permute-start.4 = (bf16[2,48,1536]{2,1,0:T(8,128)(2,1)S(1)}, bf16[2,48,1536]{2,1,0:T(8,128)(2,1)S(1)}, u32[]{:S(2)}, u32[]{:S(2)}) collective-permute-start(bf16[2,48,1536]{2,1,0:T(8,128)(2,1)S(1)} %collective-permute-done.3), channel_id=1, source_target_pairs={{0,16},{16,32},{32,48},{48,64},{64,80},{80,96},{96,112},{112,128},... | collective-permute-start | bytes 884744 | tf_op jit(solution)/shard_map/ppermute | solution.py:34
  53.7 7.4 %collective-permute-start.5 = (bf16[2,48,1536]{2,1,0:T(8,128)(2,1)S(1)}, bf16[2,48,1536]{2,1,0:T(8,128)(2,1)S(1)}, u32[]{:S(2)}, u32[]{:S(2)}) collective-permute-start(bf16[2,48,1536]{2,1,0:T(8,128)(2,1)S(1)} %collective-permute-done.4), channel_id=1, source_target_pairs={{0,16},{16,32},{32,48},{48,64},{64,80},{80,96},{96,112},{112,128},... | collective-permute-start | bytes 884744 | tf_op jit(solution)/shard_map/ppermute | solution.py:34
  61.7 7.4 %collective-permute-start.6 = (bf16[2,48,1536]{2,1,0:T(8,128)(2,1)S(1)}, bf16[2,48,1536]{2,1,0:T(8,128)(2,1)S(1)}, u32[]{:S(2)}, u32[]{:S(2)}) collective-permute-start(bf16[2,48,1536]{2,1,0:T(8,128)(2,1)S(1)} %collective-permute-done.5), channel_id=1, source_target_pairs={{0,16},{16,32},{32,48},{48,64},{64,80},{80,96},{96,112},{112,128},... | collective-permute-start | bytes 884744 | tf_op jit(solution)/shard_map/ppermute | solution.py:34
  69.8 7.4 %collective-permute-start.7 = (bf16[2,48,1536]{2,1,0:T(8,128)(2,1)S(1)}, bf16[2,48,1536]{2,1,0:T(8,128)(2,1)S(1)}, u32[]{:S(2)}, u32[]{:S(2)}) collective-permute-start(bf16[2,48,1536]{2,1,0:T(8,128)(2,1)S(1)} %collective-permute-done.6), channel_id=1, source_target_pairs={{0,16},{16,32},{32,48},{48,64},{64,80},{80,96},{96,112},{112,128},... | collective-permute-start | bytes 884744 | tf_op jit(solution)/shard_map/ppermute | solution.py:34
  77.9 7.4 %collective-permute-start.8 = (bf16[2,48,1536]{2,1,0:T(8,128)(2,1)S(1)}, bf16[2,48,1536]{2,1,0:T(8,128)(2,1)S(1)}, u32[]{:S(2)}, u32[]{:S(2)}) collective-permute-start(bf16[2,48,1536]{2,1,0:T(8,128)(2,1)S(1)} %collective-permute-done.7), channel_id=1, source_target_pairs={{0,16},{16,32},{32,48},{48,64},{64,80},{80,96},{96,112},{112,128},... | collective-permute-start | bytes 884744 | tf_op jit(solution)/shard_map/ppermute | solution.py:34
  86.0 7.4 %collective-permute-start.9 = (bf16[2,48,1536]{2,1,0:T(8,128)(2,1)S(1)}, bf16[2,48,1536]{2,1,0:T(8,128)(2,1)S(1)}, u32[]{:S(2)}, u32[]{:S(2)}) collective-permute-start(bf16[2,48,1536]{2,1,0:T(8,128)(2,1)S(1)} %collective-permute-done.8), channel_id=1, source_target_pairs={{0,16},{16,32},{32,48},{48,64},{64,80},{80,96},{96,112},{112,128},... | collective-permute-start | bytes 884744 | tf_op jit(solution)/shard_map/ppermute | solution.py:34
  94.1 7.4 %collective-permute-start.10 = (bf16[2,48,1536]{2,1,0:T(8,128)(2,1)S(1)}, bf16[2,48,1536]{2,1,0:T(8,128)(2,1)S(1)}, u32[]{:S(2)}, u32[]{:S(2)}) collective-permute-start(bf16[2,48,1536]{2,1,0:T(8,128)(2,1)S(1)} %collective-permute-done.9), channel_id=1, source_target_pairs={{0,16},{16,32},{32,48},{48,64},{64,80},{80,96},{96,112},{112,128},... | collective-permute-start | bytes 884744 | tf_op jit(solution)/shard_map/ppermute | solution.py:34
  102.1 7.4 %collective-permute-start.11 = (bf16[2,48,1536]{2,1,0:T(8,128)(2,1)S(1)}, bf16[2,48,1536]{2,1,0:T(8,128)(2,1)S(1)}, u32[]{:S(2)}, u32[]{:S(2)}) collective-permute-start(bf16[2,48,1536]{2,1,0:T(8,128)(2,1)S(1)} %collective-permute-done.10), channel_id=1, source_target_pairs={{0,16},{16,32},{32,48},{48,64},{64,80},{80,96},{96,112},{112,128},... | collective-permute-start | bytes 884744 | tf_op jit(solution)/shard_map/ppermute | solution.py:34
  110.2 7.4 %collective-permute-start.12 = (bf16[2,48,1536]{2,1,0:T(8,128)(2,1)S(1)}, bf16[2,48,1536]{2,1,0:T(8,128)(2,1)S(1)}, u32[]{:S(2)}, u32[]{:S(2)}) collective-permute-start(bf16[2,48,1536]{2,1,0:T(8,128)(2,1)S(1)} %collective-permute-done.11), channel_id=1, source_target_pairs={{0,16},{16,32},{32,48},{48,64},{64,80},{80,96},{96,112},{112,128},... | collective-permute-start | bytes 884744 | tf_op jit(solution)/shard_map/ppermute | solution.py:34
  118.3 7.5 %collective-permute-start.13 = (bf16[2,48,1536]{2,1,0:T(8,128)(2,1)S(1)}, bf16[2,48,1536]{2,1,0:T(8,128)(2,1)}, u32[]{:S(2)}, u32[]{:S(2)}) collective-permute-start(bf16[2,48,1536]{2,1,0:T(8,128)(2,1)S(1)} %collective-permute-done.12), channel_id=1, source_target_pairs={{0,16},{16,32},{32,48},{48,64},{64,80},{80,96},{96,112},{112,128},... | collective-permute-start | bytes 884744 | tf_op jit(solution)/shard_map/ppermute | solution.py:34
  125.7 7.7 %collective-permute-start.14 = (bf16[2,48,1536]{2,1,0:T(8,128)(2,1)}, bf16[2,48,1536]{2,1,0:T(8,128)(2,1)}, u32[]{:S(2)}, u32[]{:S(2)}) collective-permute-start(bf16[2,48,1536]{2,1,0:T(8,128)(2,1)} %collective-permute-done.13), channel_id=1, source_target_pairs={{0,16},{16,32},{32,48},{48,64},{64,80},{80,96},{96,112},{112,128},... | collective-permute-start | bytes 884744 | tf_op jit(solution)/shard_map/ppermute | solution.py:34
  125.8 24.7 %copy-start.10 = (bf16[2,48,1536]{2,1,0:T(8,128)(2,1)S(1)}, bf16[2,48,1536]{2,1,0:T(8,128)(2,1)}, u32[]{:S(2)}) copy-start(bf16[2,48,1536]{2,1,0:T(8,128)(2,1)} %copy-done.9) | copy-start | bytes 884740
  125.8 24.7 %copy-start.8 = (bf16[2,48,1536]{2,1,0:T(8,128)(2,1)S(1)}, bf16[2,48,1536]{2,1,0:T(8,128)(2,1)}, u32[]{:S(2)}) copy-start(bf16[2,48,1536]{2,1,0:T(8,128)(2,1)} %copy-done.7) | copy-start | bytes 884740
  125.8 24.8 %copy-start.6 = (bf16[2,48,1536]{2,1,0:T(8,128)(2,1)S(1)}, bf16[2,48,1536]{2,1,0:T(8,128)(2,1)}, u32[]{:S(2)}) copy-start(bf16[2,48,1536]{2,1,0:T(8,128)(2,1)} %copy-done.5) | copy-start | bytes 884740
  125.8 24.8 %copy-start.4 = (bf16[2,48,1536]{2,1,0:T(8,128)(2,1)S(1)}, bf16[2,48,1536]{2,1,0:T(8,128)(2,1)}, u32[]{:S(2)}) copy-start(bf16[2,48,1536]{2,1,0:T(8,128)(2,1)} %copy-done.3) | copy-start | bytes 884740
  125.8 24.8 %copy-start.2 = (bf16[2,48,1536]{2,1,0:T(8,128)(2,1)S(1)}, bf16[2,48,1536]{2,1,0:T(8,128)(2,1)}, u32[]{:S(2)}) copy-start(bf16[2,48,1536]{2,1,0:T(8,128)(2,1)} %copy-done.1) | copy-start | bytes 884740
  125.9 24.9 %copy-start.28 = (bf16[2,1536,512]{2,1,0:T(8,128)(2,1)S(1)}, bf16[2,1536,512]{2,1,0:T(8,128)(2,1)}, u32[]{:S(2)}) copy-start(bf16[2,1536,512]{2,1,0:T(8,128)(2,1)} %param.9) | copy-start | bytes 9437188
  159.4 213.6 %reduce-scatter.2.cloned.1.call-start = ((), (), s32[]{:S(2)}) async-start(), calls=%async_computation.2 | async-start | bytes 10027008 | tf_op jit(solution)/shard_map/reduce_scatter | solution.py:45
  (23 other events, 209.4 us)
Sparse Core Ops, SparseCore 0:
  159.5 131.5 all-reduce.2
  299.4 73.6 reduce-scatter.1
